TPU v7x, 32 devices: a whole 2x2x4 slice. The times are simulated.
32 devices in a mesh: groups: 2 (over x), ctx: 16 (over z, y, core).
Axes of the slice: x: 2, y: 2, z: 4, core: 2. Of those that a mesh axis runs over, the one named last changes fastest.
Arguments:
- query_rows: bfloat16 [8192, 1024], P(('groups', 'ctx')), parts along dimension 0, may hold values from -6 to 6
- key_rows: bfloat16 [8192, 1024], P(('groups', 'ctx')), parts along dimension 0, may hold values from -6 to 6
- value_rows: bfloat16 [8192, 1024], P(('groups', 'ctx')), parts along dimension 0, may hold values from -6 to 6
- out_grad: bfloat16 [8192, 1024], P(('groups', 'ctx')), parts along dimension 0, may hold values from -6 to 6
Outputs:
- attended: bfloat16 [8192, 1024], P(('groups', 'ctx')), parts along dimension 0
- query_grad: bfloat16 [8192, 1024], P(('groups', 'ctx')), parts along dimension 0
- key_grad: bfloat16 [8192, 1024], P(('groups', 'ctx')), parts along dimension 0
- value_grad: bfloat16 [8192, 1024], P(('groups', 'ctx')), parts along dimension 0
There are 2 independent parts, one for each index of `groups`. A program takes and returns all parts, laid end to end along the dimension named above; each array names one. Nothing has to cross between parts.
All inputs are finite; a program needn't handle non-finite values.
Results may differ from a plain program's by a relative error of at most 0.0059.
Values sent between devices are 32-bit elements; how exact they have to be, the bound alone decides.
A program may use at most 320 MiB of HBM per device.

v0:
```python
import jax
import jax.numpy as jnp
from jax import lax
from jax.sharding import PartitionSpec as P

HEADS = 8
DH = 128


def prefix_2(shard, axis, combine, identity, reverse):
    devices, here = (lax.axis_size(axis), lax.axis_index(axis))
    everything = lax.all_gather(shard, axis)
    start = jnp.broadcast_to(jnp.asarray(identity, shard.dtype), shard.shape)

    def turn(k, before):
        at = devices - 1 - k if reverse else k
        reached = at > here if reverse else at < here
        new = combine(before, everything[at])
        return jnp.where(reached, new, before)

    return lax.fori_loop(0, devices, turn, start)


def add_states(earlier, later):
    return earlier + later


def body(query_rows, key_rows, value_rows, out_grad):
    tokens = query_rows.shape[0]
    shape3 = (tokens, HEADS, DH)
    queries = query_rows.reshape(shape3)
    key_block = key_rows.reshape(shape3)
    value_block = value_rows.reshape(shape3)
    start = lax.axis_index("ctx") * tokens
    positions = (start + lax.iota(jnp.int32, tokens)).astype(jnp.float32)
    row_scale = (1.0 / jnp.sqrt(DH * (positions + 1.0))).reshape(tokens, 1, 1)
    scaled_grad = (row_scale * out_grad.reshape(shape3).astype(jnp.float32)).astype(jnp.bfloat16)
    kv_state = jnp.einsum(
        "thd,the->hde", key_block, value_block, preferred_element_type=jnp.float32
    )
    qg_state = jnp.einsum("thd,the->hde", queries, scaled_grad, preferred_element_type=jnp.float32)
    zero_state = jnp.zeros_like(kv_state)
    prefix = prefix_2(kv_state, "ctx", add_states, zero_state, False)
    suffix = prefix_2(qg_state, "ctx", add_states, zero_state, True)
    prefix_low = prefix.astype(jnp.bfloat16)
    suffix_low = suffix.astype(jnp.bfloat16)
    causal_mask = jnp.tril(jnp.ones((tokens, tokens), dtype=bool))[None]
    scores = jnp.einsum("thd,shd->hts", queries, key_block, preferred_element_type=jnp.float32)
    scores = jnp.where(causal_mask, scores, 0.0).astype(jnp.bfloat16)
    dscores = jnp.einsum(
        "the,she->hts", scaled_grad, value_block, preferred_element_type=jnp.float32
    )
    dscores = jnp.where(causal_mask, dscores, 0.0).astype(jnp.bfloat16)
    attended = row_scale * (
        jnp.einsum("hts,she->the", scores, value_block, preferred_element_type=jnp.float32)
        + jnp.einsum("thd,hde->the", queries, prefix_low, preferred_element_type=jnp.float32)
    )
    query_grad = jnp.einsum(
        "hts,shd->thd", dscores, key_block, preferred_element_type=jnp.float32
    ) + jnp.einsum("the,hde->thd", scaled_grad, prefix_low, preferred_element_type=jnp.float32)
    key_grad = jnp.einsum(
        "hts,thd->shd", dscores, queries, preferred_element_type=jnp.float32
    ) + jnp.einsum("she,hde->shd", value_block, suffix_low, preferred_element_type=jnp.float32)
    value_grad = jnp.einsum(
        "hts,the->she", scores, scaled_grad, preferred_element_type=jnp.float32
    ) + jnp.einsum("shd,hde->she", key_block, suffix_low, preferred_element_type=jnp.float32)
    width = HEADS * DH
    return (
        attended.astype(jnp.bfloat16).reshape(tokens, width),
        query_grad.astype(jnp.bfloat16).reshape(tokens, width),
        key_grad.astype(jnp.bfloat16).reshape(tokens, width),
        value_grad.astype(jnp.bfloat16).reshape(tokens, width),
    )


def solution(mesh):
    in_specs = (
        P(("groups", "ctx"), None),
        P(("groups", "ctx"), None),
        P(("groups", "ctx"), None),
        P(("groups", "ctx"), None),
    )
    out_specs = (
        P(("groups", "ctx"), None),
        P(("groups", "ctx"), None),
        P(("groups", "ctx"), None),
        P(("groups", "ctx"), None),
    )
    return jax.shard_map(body, mesh=mesh, in_specs=in_specs, out_specs=out_specs, check_vma=False)
```

profile of v0, /device:TPU:0, one launch (start us, length us, event | category | flops | bytes accessed | tf_op | source)
XLA Modules:
  0.0 200.5 jit_solution(14173594211373190287)
XLA Ops:
  13.8 1.5 convolution_bitcast_fusion.4
  15.2 1.4 convolution_bitcast_fusion.3
  16.6 1.3 fusion.33
  17.9 1.5 convolution_bitcast_fusion.5
  19.4 69.0 %all-gather.5.cloned.1.call-done = f32[128,128,128]{2,1,0:T(8,128)} async-done(((f32[8,128,128]{2,1,0:T(8,128)}), f32[128,128,128]{2,1,0:T(8,128)}) %all-gather.5.cloned.1.call-update) | async-done | bytes 8388624 | tf_op jit(solution)/shard_map/all_gather | solution.py:12
  88.4 20.1 %while.30 = (s32[]{:T(128)}, f32[8,128,128]{2,1,0:T(8,128)S(1)}, s32[]{:T(128)}, f32[16,8,128,128]{3,2,1,0:T(8,128)}, s32[]{:T(128)}, /*index=5*/s32[]{:T(128)}) while((s32[]{:T(128)}, f32[8,128,128]{2,1,0:T(8,128)S(1)}, s32[]{:T(128)}, f32[16,8,128,128]{3,2,1,0:T(8,128)}, s32[]{:T(128)}, /*index=5*/s32[]{:T(128)}) %tuple.85), condition=%wide.region_1.2_spmd.clone, body=%wide.region_0.1_spmd.clone.sunk | while | flops 393220 | bytes 1572957 | solution.py:21
  89.6 1.2 add_select_fusion.4
  90.9 1.2 add_select_fusion.4
  92.1 1.2 add_select_fusion.4
  93.4 1.2 add_select_fusion.4
  95.9 1.3 add_select_fusion.4
  97.2 1.2 add_select_fusion.4
  99.7 1.2 add_select_fusion.4
  102.2 1.2 add_select_fusion.4
  103.4 1.2 add_select_fusion.4
  108.4 1.5 fusion.5
  111.0 53.3 %all-gather.7.cloned.1.call-done = f32[128,128,128]{2,1,0:T(8,128)} async-done(((f32[8,128,128]{2,1,0:T(8,128)}), f32[128,128,128]{2,1,0:T(8,128)}) %all-gather.7.cloned.1.call-update) | async-done | bytes 8388624 | tf_op jit(solution)/shard_map/all_gather | solution.py:12
  164.3 20.2 %while.31 = (s32[]{:T(128)}, f32[8,128,128]{2,1,0:T(8,128)S(1)}, s32[]{:T(128)}, f32[16,8,128,128]{3,2,1,0:T(8,128)}, s32[]{:T(128)}, /*index=5*/s32[]{:T(128)}, s32[]{:T(128)}, s32[]{:T(128)}) while((s32[]{:T(128)}, f32[8,128,128]{2,1,0:T(8,128)S(1)}, s32[]{:T(128)}, f32[16,8,128,128]{3,2,1,0:T(8,128)}, s32[]{:T(128)}, ...), condition=%wide.region_3.4_spmd.clone, body=%wide.region_2.3_spmd.clone.sunk | while | flops 393224 | bytes 1573019 | solution.py:21
  164.3 1.3 add_select_fusion.5
  168.2 1.2 add_select_fusion.5
  177.0 1.2 add_select_fusion.5
  185.6 2.0 %copy.50 = bf16[256,1024]{1,0:T(8,128)(2,1)} copy(bf16[256,1024]{0,1:T(8,128)(2,1)} %bitcast.118) | data formatting | bytes 1048576
  187.6 2.6 %fusion.7 = bf16[8,128,256]{2,1,0:T(8,128)(2,1)} fusion(f32[8,128,256]{2,1,0:T(8,128)} %fusion.33, f32[8,128,128]{2,1,0:T(8,128)S(1)} %get-tuple-element.194, bf16[256,1024]{1,0:T(8,128)(2,1)} %param.9), kind=kOutput, calls=%fused_computation.18 | convolution fusion | flops 67764224 | bytes 2621440 | tf_op jit(solution)/shard_map/shd,hde->she/dot_general | solution.py:66
  190.3 2.0 %copy.51 = bf16[256,1024]{1,0:T(8,128)(2,1)} copy(bf16[256,1024]{0,1:T(8,128)(2,1)} %bitcast.117) | data formatting | bytes 1048576
  (53 shorter events, 34.4 us)
Async XLA Ops:
  7.2 1.6 copy-start
  7.2 81.2 %all-gather.5.cloned.1.call-start = ((), (), s32[]{:S(2)}) async-start(), calls=%async_computation | async-start | bytes 8912896 | tf_op jit(solution)/shard_map/all_gather | solution.py:12
  7.2 2.7 %copy-start.5 = (bf16[256,1024]{1,0:T(8,128)(2,1)S(1)}, bf16[256,1024]{1,0:T(8,128)(2,1)}, u32[]{:S(2)}) copy-start(bf16[256,1024]{1,0:T(8,128)(2,1)} %param.11) | copy-start | bytes 1572868
  9.9 1.0 copy-start.1
  9.9 154.4 %all-gather.7.cloned.1.call-start = ((), (), s32[]{:S(2)}) async-start(), calls=%async_computation.1 | async-start | bytes 8912896 | tf_op jit(solution)/shard_map/all_gather | solution.py:12
  12.3 1.0 copy-start.4
  164.3 20.2 %copy-start.3 = (f32[256,8,128]{0,2,1:T(8,128)S(1)}, f32[256,8,128]{0,2,1:T(8,128)}, u32[]{:S(2)}) copy-start(f32[256,8,128]{0,2,1:T(8,128)} %convolution_bitcast_fusion.3) | copy-start | bytes 3145732
  187.6 4.7 %copy-start.2 = (f32[256,8,128]{0,2,1:T(8,128)S(1)}, f32[256,8,128]{0,2,1:T(8,128)}, u32[]{:S(2)}) copy-start(f32[256,8,128]{0,2,1:T(8,128)} %convolution_bitcast_fusion.5) | copy-start | bytes 3145732
Sparse Core Ops, SparseCore 0:
  10.7 77.5 all-gather.4
  91.1 73.1 all-gather.6
where the time goes:
time: 202 us; the launch traced here: 200 us
  waiting for transfers between devices  122 us (60%)
  other arithmetic  39.5 us (20%)
  between operations  14.2 us (7%)
  matrix products  13.5 us (7%)
  local copies, waits for them, and re-layouts  9.97 us (5%)
    all_gather x2, waiting for transfers between devices, prefix_2(): everything = lax.all_gather(shard, axis)  122 us
    select_n x32, other arithmetic, turn(): return jnp.where(reached, new, before)  39.4 us
    unnamed x17, local copies, waits for them, and re-layouts  8.45 us
  transfers between devices with their start and end apart: 2, of which 2 were waited for; matrix products, arithmetic and copies ran while one was open for 15% of the time, Pallas kernels for 0%

commit v1 on v0

v1 whole, which is shorter than its diff:
```python
import functools

import jax
import jax.numpy as jnp
from jax import lax
from jax.experimental import pallas as pl
from jax.experimental.pallas import tpu as pltpu
from jax.sharding import PartitionSpec as P

DH = 128
MESH = pl.DeviceIdType.MESH
F32 = jnp.float32
BF16 = jnp.bfloat16


def dot(a, b, ca, cb):
    return lax.dot_general(a, b, (((ca,), (cb,)), ((), ())), preferred_element_type=F32)


def kernel(
    planes,
    heads,
    q_hbm,
    k_hbm,
    v_hbm,
    do_hbm,
    att_ref,
    qg_ref,
    kg_ref,
    vg_ref,
    q_ref,
    k_ref,
    v_ref,
    do_ref,
    g_ref,
    state,
    sib_in,
    y_out,
    y_in,
    z_out,
    z_in,
    ret_out,
    total,
    acc_a,
    acc_q,
    acc_k,
    acc_v,
    load_sem,
    sib_s,
    sib_r,
    y_s,
    y_r,
    z_s,
    z_r,
    ret_s,
    ret_r,
):
    tokens = q_ref.shape[0]
    group = lax.axis_index("groups")
    me = lax.axis_index("ctx")
    core = lax.rem(me, 2)
    row = lax.rem(me // 2, 2)
    plane = me // 4
    other = 1 - core
    step = 4 * (1 - 2 * core)
    has_prev = jnp.where(core == 0, plane > 0, plane < planes - 1)
    has_next = jnp.where(core == 0, plane < planes - 1, plane > 0)
    sibling = me + 1 - 2 * core
    partner = me + 2 - 4 * row
    is_low = row == core
    low = jnp.where(is_low, 1.0, 0.0).astype(F32)
    high = 1.0 - low

    def cols(h):
        return pl.ds(h * DH, DH)

    barrier = pltpu.get_barrier_semaphore()
    for device in (sibling, partner):
        pl.semaphore_signal(barrier, inc=1, device_id=(group, device), device_id_type=MESH)

    @pl.when(has_prev)
    def _():
        pl.semaphore_signal(barrier, inc=1, device_id=(group, me - step), device_id_type=MESH)

    @pl.when(has_next)
    def _():
        pl.semaphore_signal(barrier, inc=1, device_id=(group, me + step), device_id_type=MESH)

    first = heads // 2
    order = [h for i in range(first) for h in (i, first + i)]
    if heads % 2:
        order.append(heads - 1)

    loads = {}
    for h in order:
        for i, (src, dst) in enumerate(
            ((q_hbm, q_ref), (k_hbm, k_ref), (v_hbm, v_ref), (do_hbm, do_ref))
        ):
            loads[h, i] = pltpu.make_async_copy(
                src.at[:, cols(h)], dst.at[:, cols(h)], load_sem.at[i, h]
            )
            loads[h, i].start()

    @pl.when(jnp.logical_not(has_prev))
    def _():
        z_in[...] = jnp.zeros_like(z_in)

    def remote(src, dst, send, recv, device):
        return pltpu.make_async_remote_copy(
            src_ref=src,
            dst_ref=dst,
            send_sem=send,
            recv_sem=recv,
            device_id=(group, device),
            device_id_type=MESH,
        )

    def sib_copy(h):
        return remote(state.at[other, h], sib_in.at[h], sib_s.at[h], sib_r.at[h], sibling)

    def y_copy(h):
        return remote(y_out.at[h], y_in.at[h], y_s.at[h], y_r.at[h], partner)

    def z_copy(h):
        return remote(z_out.at[h], z_in.at[h], z_s.at[h], z_r.at[h], me + step)

    def ret_copy(h):
        return remote(ret_out.at[h], total.at[core, h], ret_s.at[h], ret_r.at[h], sibling)

    position = (me * tokens + lax.broadcasted_iota(jnp.int32, (tokens, DH), 0)).astype(F32)
    scale = 1.0 / jnp.sqrt(DH * (position + 1.0))

    for n, h in enumerate(order):
        for i in range(4):
            loads[h, i].wait()
        g = (scale * do_ref[:, cols(h)].astype(F32)).astype(BF16)
        g_ref[:, cols(h)] = g
        state[0, h] = dot(k_ref[:, cols(h)], v_ref[:, cols(h)], 0, 0)
        state[1, h] = dot(q_ref[:, cols(h)], g, 0, 0)
        if n == 0:
            pl.semaphore_wait(
                barrier, 2 + has_prev.astype(jnp.int32) + has_next.astype(jnp.int32)
            )
        sib_copy(h).start()

    def local(h):
        c = cols(h)
        q, k, v, g = q_ref[:, c], k_ref[:, c], v_ref[:, c], g_ref[:, c]
        t = lax.broadcasted_iota(jnp.int32, (tokens, tokens), 0)
        s = lax.broadcasted_iota(jnp.int32, (tokens, tokens), 1)
        scores = jnp.where(t >= s, dot(q, k, 1, 1), 0.0).astype(BF16)
        dscores = jnp.where(t >= s, dot(g, v, 1, 1), 0.0).astype(BF16)
        acc_a[:, c] = dot(scores, v, 1, 0)
        acc_q[:, c] = dot(dscores, k, 1, 0)
        acc_k[:, c] = dot(dscores, q, 0, 0)
        acc_v[:, c] = dot(scores, g, 0, 0)

    for h in order:
        sib_copy(h).wait_recv()
        if h < first:
            y_out[h] = state[core, h] + sib_in[h]
            y_copy(h).start()

    def give(h, base):
        total[core, h] = base
        ret_out[h] = base + state[core, h]
        ret_copy(h).start()

    def wait_plane(h):
        @pl.when(has_prev)
        def _():
            z_copy(h).wait_recv()

    def send_plane(h):
        @pl.when(has_next)
        def _():
            z_copy(h).start()

    for h in range(first, heads):
        wait_plane(h)
        here = state[core, h] + sib_in[h]
        z_out[h] = z_in[h] + here
        send_plane(h)
        y_out[h] = z_in[h] + low * here
        y_copy(h).start()
        local(h)

    for h in range(first):
        y_copy(h).wait_recv()
        wait_plane(h)
        before = z_in[h]
        z_out[h] = before + (y_out[h] + y_in[h])
        send_plane(h)
        give(h, before + high * y_in[h])
        local(h)

    for h in range(first, heads):
        y_copy(h).wait_recv()
        give(h, z_in[h] + y_in[h])

    for h in range(heads):
        ret_copy(h).wait_recv()
        c = cols(h)
        q, k, v, g = q_ref[:, c], k_ref[:, c], v_ref[:, c], g_ref[:, c]
        prefix = total[0, h].astype(BF16)
        suffix = total[1, h].astype(BF16)
        att_ref[:, c] = (scale * (acc_a[:, c] + dot(q, prefix, 1, 0))).astype(BF16)
        qg_ref[:, c] = (acc_q[:, c] + dot(g, prefix, 1, 1)).astype(BF16)
        kg_ref[:, c] = (acc_k[:, c] + dot(v, suffix, 1, 1)).astype(BF16)
        vg_ref[:, c] = (acc_v[:, c] + dot(k, suffix, 1, 0)).astype(BF16)

    for h in range(heads):
        sib_copy(h).wait_send()
        y_copy(h).wait_send()
        ret_copy(h).wait_send()

        @pl.when(has_next)
        def _():
            z_copy(h).wait_send()


def body(planes, query_rows, key_rows, value_rows, out_grad):
    tokens, width = query_rows.shape
    heads = width // DH
    out = jax.ShapeDtypeStruct((tokens, width), BF16)
    mat = pltpu.VMEM((heads, DH, DH), F32)
    mat2 = pltpu.VMEM((2, heads, DH, DH), F32)
    rows16 = pltpu.VMEM((tokens, width), BF16)
    rows32 = pltpu.VMEM((tokens, width), F32)
    sem = pltpu.SemaphoreType.DMA((heads,))
    return pl.pallas_call(
        functools.partial(kernel, planes, heads),
        out_shape=[out] * 4,
        in_specs=[pl.BlockSpec(memory_space=pl.ANY)] * 4,
        out_specs=[pl.BlockSpec(memory_space=pltpu.VMEM)] * 4,
        scratch_shapes=[rows16] * 5
        + [mat2, mat, mat, mat, mat, mat, mat, mat2]
        + [rows32] * 4
        + [pltpu.SemaphoreType.DMA((4, heads))]
        + [sem] * 8,
        compiler_params=pltpu.CompilerParams(
            collective_id=0, has_side_effects=True, vmem_limit_bytes=40 * 1024 * 1024
        ),
        cost_estimate=pl.CostEstimate(
            flops=18 * tokens * tokens * width, bytes_accessed=16 * tokens * width, transcendentals=0
        ),
    )(query_rows, key_rows, value_rows, out_grad)


def solution(mesh):
    spec = P(("groups", "ctx"), None)
    return jax.shard_map(
        functools.partial(body, mesh.shape["ctx"] // 4),
        mesh=mesh,
        in_specs=(spec,) * 4,
        out_specs=(spec,) * 4,
        check_vma=False,
    )
```

time: 202 us -> 32.1 us (0.16)
  waiting for transfers between devices: 122 us -> 0 us
  other arithmetic: 39.5 us -> 0 us
  Pallas kernels: 0 us -> 23.8 us
  between operations: 14.2 us -> 0.65 us
  matrix products: 13.5 us -> 0 us
  local copies, waits for them, and re-layouts: 9.97 us -> 7.33 us
    all_gather x2 -> x0, waiting for transfers between devices: 122 us -> none  [prefix_2(): everything = lax.all_gather(shard, axis)]
    select_n x32 -> x0, other arithmetic: 39.4 us -> none  [turn(): return jnp.where(reached, new, before)]
    pallas_call x0 -> x1, Pallas kernels: none -> 23.8 us  [body(): pl.pallas_call(functools.partial(kernel, planes, heads), out_shape=[out]...]
    dot_general x12 -> x0, matrix products: 13.5 us -> none  [the longest x1 2.61 us: body(): jnp.einsum('shd,hde->she', key_block, suffix_low, preferred_element_type=...]
    unnamed x17 -> x12, local copies, waits for them, and re-layouts: 8.45 us -> 7.33 us
  transfers between devices with their start and end apart: 2 -> 0, of which waited for: 2 -> 0; matrix products, arithmetic and copies ran while one was open for 15% -> 0% of each run, Pallas kernels for 0% -> 0%
where the time goes in v1:
time: 32.1 us; the launch traced here: 31.8 us
  Pallas kernels  23.8 us (74%)
  local copies, waits for them, and re-layouts  7.33 us (23%)
  between operations  0.65 us (2%)
    pallas_call x1, Pallas kernels, body(): pl.pallas_call(functools.partial(kernel, planes, heads), out_shape=[out]...  23.8 us
    unnamed x12, local copies, waits for them, and re-layouts  7.33 us

profile of v1, /device:TPU:0, one launch (start us, length us, event | category | flops | bytes accessed | tf_op | source)
XLA Modules:
  0.0 31.8 jit_solution(18271336060743845487)
XLA Ops:
  0.6 0.0 copy-start
  0.6 1.0 %copy-done = bf16[256,1024]{1,0:T(8,128)(2,1)S(1)} copy-done((bf16[256,1024]{1,0:T(8,128)(2,1)S(1)}, bf16[256,1024]{1,0:T(8,128)(2,1)}, u32[]{:S(2)}) %copy-start) | copy-done | bytes 524312
  1.7 0.0 copy-start.1
  1.7 1.0 %copy-done.1 = bf16[256,1024]{1,0:T(8,128)(2,1)S(1)} copy-done((bf16[256,1024]{1,0:T(8,128)(2,1)S(1)}, bf16[256,1024]{1,0:T(8,128)(2,1)}, u32[]{:S(2)}) %copy-start.1) | copy-done | bytes 524312
  2.7 0.0 copy-start.2
  2.7 1.0 %copy-done.2 = bf16[256,1024]{1,0:T(8,128)(2,1)S(1)} copy-done((bf16[256,1024]{1,0:T(8,128)(2,1)S(1)}, bf16[256,1024]{1,0:T(8,128)(2,1)}, u32[]{:S(2)}) %copy-start.2) | copy-done | bytes 524312
  3.8 0.0 copy-start.3
  3.8 1.0 %copy-done.3 = bf16[256,1024]{1,0:T(8,128)(2,1)S(1)} copy-done((bf16[256,1024]{1,0:T(8,128)(2,1)S(1)}, bf16[256,1024]{1,0:T(8,128)(2,1)}, u32[]{:S(2)}) %copy-start.3) | copy-done | bytes 524312
  4.8 23.8 %shard_map.75 = (bf16[256,1024]{1,0:T(8,128)(2,1)S(1)}, bf16[256,1024]{1,0:T(8,128)(2,1)S(1)}, bf16[256,1024]{1,0:T(8,128)(2,1)S(1)}, bf16[256,1024]{1,0:T(8,128)(2,1)S(1)}) custom-call(bf16[256,1024]{1,0:T(8,128)(2,1)S(1)} %copy-done, bf16[256,1024]{1,0:T(8,128)(2,1)S(1)} %copy-done.1, bf16[256,1024]{1,0:T(8,128)(2,1)S(1)} %copy-done.2, ...), custom_call_target="tpu_custom_call" | custom-call | flops 1207959552 | bytes 4194304 | tf_op jit(solution)/shard_map/pallas_call | solution.py:231
  28.6 0.8 %copy.12 = bf16[256,1024]{1,0:T(8,128)(2,1)} copy(bf16[256,1024]{1,0:T(8,128)(2,1)S(1)} %get-tuple-element.8) | data formatting | bytes 1048576
  29.4 0.8 %copy.13 = bf16[256,1024]{1,0:T(8,128)(2,1)} copy(bf16[256,1024]{1,0:T(8,128)(2,1)S(1)} %get-tuple-element.9) | data formatting | bytes 1048576
  30.2 0.8 %copy.14 = bf16[256,1024]{1,0:T(8,128)(2,1)} copy(bf16[256,1024]{1,0:T(8,128)(2,1)S(1)} %get-tuple-element.10) | data formatting | bytes 1048576
  31.0 0.8 %copy.15 = bf16[256,1024]{1,0:T(8,128)(2,1)} copy(bf16[256,1024]{1,0:T(8,128)(2,1)S(1)} %get-tuple-element.11) | data formatting | bytes 1048576
Async XLA Ops:
  0.6 1.0 %copy-start = (bf16[256,1024]{1,0:T(8,128)(2,1)S(1)}, bf16[256,1024]{1,0:T(8,128)(2,1)}, u32[]{:S(2)}) copy-start(bf16[256,1024]{1,0:T(8,128)(2,1)} %q_hbm.1) | copy-start | bytes 1572868
  1.7 1.0 %copy-start.1 = (bf16[256,1024]{1,0:T(8,128)(2,1)S(1)}, bf16[256,1024]{1,0:T(8,128)(2,1)}, u32[]{:S(2)}) copy-start(bf16[256,1024]{1,0:T(8,128)(2,1)} %k_hbm.1) | copy-start | bytes 1572868
  2.7 1.0 %copy-start.2 = (bf16[256,1024]{1,0:T(8,128)(2,1)S(1)}, bf16[256,1024]{1,0:T(8,128)(2,1)}, u32[]{:S(2)}) copy-start(bf16[256,1024]{1,0:T(8,128)(2,1)} %v_hbm.1) | copy-start | bytes 1572868
  3.8 1.0 %copy-start.3 = (bf16[256,1024]{1,0:T(8,128)(2,1)S(1)}, bf16[256,1024]{1,0:T(8,128)(2,1)}, u32[]{:S(2)}) copy-start(bf16[256,1024]{1,0:T(8,128)(2,1)} %do_hbm.1) | copy-start | bytes 1572868

commit v2 on v1

--- a/solution.py
+++ b/solution.py
@@ -194,11 +194,7 @@
         give(h, before + high * y_in[h])
         local(h)
 
-    for h in range(first, heads):
-        y_copy(h).wait_recv()
-        give(h, z_in[h] + y_in[h])
-
-    for h in range(heads):
+    def finish(h):
         ret_copy(h).wait_recv()
         c = cols(h)
         q, k, v, g = q_ref[:, c], k_ref[:, c], v_ref[:, c], g_ref[:, c]
@@ -209,6 +205,15 @@
         kg_ref[:, c] = (acc_k[:, c] + dot(v, suffix, 1, 1)).astype(BF16)
         vg_ref[:, c] = (acc_v[:, c] + dot(k, suffix, 1, 0)).astype(BF16)
 
+    for h in range(first, heads):
+        y_copy(h).wait_recv()
+        give(h, z_in[h] + y_in[h])
+        if h - first < first:
+            finish(h - first)
+
+    for h in range(first, heads):
+        finish(h)
+
     for h in range(heads):
         sib_copy(h).wait_send()
         y_copy(h).wait_send()
@@ -217,6 +222,17 @@
         @pl.when(has_next)
         def _():
             z_copy(h).wait_send()
+
+
+def store_kernel(a_in, q_in, k_in, v_in, a_out, q_out, k_out, v_out, sems):
+    pairs = ((a_in, a_out), (q_in, q_out), (k_in, k_out), (v_in, v_out))
+    copies = [
+        pltpu.make_async_copy(src, dst, sems.at[i]) for i, (src, dst) in enumerate(pairs)
+    ]
+    for copy in copies:
+        copy.start()
+    for copy in copies:
+        copy.wait()
 
 
 def body(planes, query_rows, key_rows, value_rows, out_grad):
@@ -228,10 +244,10 @@
     rows16 = pltpu.VMEM((tokens, width), BF16)
     rows32 = pltpu.VMEM((tokens, width), F32)
     sem = pltpu.SemaphoreType.DMA((heads,))
-    return pl.pallas_call(
+    results = pl.pallas_call(
         functools.partial(kernel, planes, heads),
         out_shape=[out] * 4,
-        in_specs=[pl.BlockSpec(memory_space=pl.ANY)] * 4,
+        in_specs=[pl.BlockSpec(memory_space=pltpu.HBM)] * 4,
         out_specs=[pl.BlockSpec(memory_space=pltpu.VMEM)] * 4,
         scratch_shapes=[rows16] * 5
         + [mat2, mat, mat, mat, mat, mat, mat, mat2]
@@ -244,7 +260,15 @@
         cost_estimate=pl.CostEstimate(
             flops=18 * tokens * tokens * width, bytes_accessed=16 * tokens * width, transcendentals=0
         ),
-    )(query_rows, key_rows, value_rows, out_grad)
+    )(*(pltpu.with_memory_space_constraint(x, pltpu.HBM) for x in (query_rows, key_rows, value_rows, out_grad)))
+    return pl.pallas_call(
+        store_kernel,
+        out_shape=[out] * 4,
+        in_specs=[pl.BlockSpec(memory_space=pltpu.VMEM)] * 4,
+        out_specs=[pl.BlockSpec(memory_space=pltpu.HBM)] * 4,
+        scratch_shapes=[pltpu.SemaphoreType.DMA((4,))],
+        compiler_params=pltpu.CompilerParams(vmem_limit_bytes=123 * 1024 * 1024 // 2),
+    )(*(pltpu.with_memory_space_constraint(x, pltpu.VMEM) for x in results))
 
 
 def solution(mesh):

time: 32.1 us -> 26.3 us (0.82)
  local copies, waits for them, and re-layouts: 7.33 us -> 0 us
  Pallas kernels: 23.8 us -> 25.5 us
    unnamed x12 -> x0, local copies, waits for them, and re-layouts: 7.33 us -> none
    pallas_call x0 -> x1, Pallas kernels: none -> 1.35 us  [body(): pl.pallas_call(store_kernel, out_shape=[out] * 4, in_specs=[pl.BlockSpec(...]
    pallas_call x1, Pallas kernels: 23.8 us -> 24.1 us  [body(): pl.pallas_call(functools.partial(kernel, planes, heads), out_shape=[out]...]
where the time goes in v2:
time: 26.3 us; the launch traced here: 26.1 us
  Pallas kernels  25.5 us (97%)
  between operations  0.64 us (2%)
    pallas_call x1, Pallas kernels, body(): pl.pallas_call(functools.partial(kernel, planes, heads), out_shape=[out]...  24.1 us
    pallas_call x1, Pallas kernels, body(): pl.pallas_call(store_kernel, out_shape=[out] * 4, in_specs=[pl.BlockSpec(...  1.35 us

profile of v2, /device:TPU:0, one launch (start us, length us, event | category | flops | bytes accessed | tf_op | source)
XLA Modules:
  0.0 26.1 jit_solution(6474308420311520077)
XLA Ops:
  0.6 24.1 %shard_map.75 = (bf16[256,1024]{1,0:T(8,128)(2,1)S(1)}, bf16[256,1024]{1,0:T(8,128)(2,1)S(1)}, bf16[256,1024]{1,0:T(8,128)(2,1)S(1)}, bf16[256,1024]{1,0:T(8,128)(2,1)S(1)}) custom-call(bf16[256,1024]{1,0:T(8,128)(2,1)} %q_hbm.1, bf16[256,1024]{1,0:T(8,128)(2,1)} %k_hbm.1, bf16[256,1024]{1,0:T(8,128)(2,1)} %v_hbm.1, bf16[256,1024]{1,0:T(8,128)(2,1)} %do_hbm.1), custom_call_target="tpu_custom_call" | custom-call | flops 1207959552 | bytes 4194304 | tf_op jit(solution)/shard_map/pallas_call | solution.py:247
  24.8 1.3 %shard_map.76 = (bf16[256,1024]{1,0:T(8,128)(2,1)}, bf16[256,1024]{1,0:T(8,128)(2,1)}, bf16[256,1024]{1,0:T(8,128)(2,1)}, bf16[256,1024]{1,0:T(8,128)(2,1)}) custom-call(bf16[256,1024]{1,0:T(8,128)(2,1)S(1)} %get-tuple-element.8.a_in, bf16[256,1024]{1,0:T(8,128)(2,1)S(1)} %get-tuple-element.9.q_in, bf16[256,1024]{1,0:T(8,128)(2,1)S(1)} %get-tuple-element.10.k_in, ...), custom_call_target="tpu_custom_call" | custom-call | tf_op jit(solution)/shard_map/pallas_call | solution.py:264

commit v3 on v2

--- a/solution.py
+++ b/solution.py
@@ -86,10 +86,18 @@
     def _():
         pl.semaphore_signal(barrier, inc=1, device_id=(group, me + step), device_id_type=MESH)
 
-    first = heads // 2
-    order = [h for i in range(first) for h in (i, first + i)]
-    if heads % 2:
-        order.append(heads - 1)
+    first = 3 * heads // 8
+    order = [h for i in range(heads) for h in (i, first + i) if i < first or h >= first]
+    order = [h for n, h in enumerate(order) if h < heads and h not in order[:n]]
+
+    last = heads - first
+    early = [[h] if h < first // 2 else [] for h in range(last)]
+    rest = []
+    for n in range(max(first, last)):
+        rest += [first + n] if n < last else []
+        rest += [first // 2 + n] if first // 2 + n < first else []
+    y_send = [(has_next if h < first else has_prev) | is_low for h in range(heads)]
+    y_recv = [(has_next if h < first else has_prev) | jnp.logical_not(is_low) for h in range(heads)]
 
     loads = {}
     for h in order:
@@ -105,6 +113,12 @@
     def _():
         z_in[...] = jnp.zeros_like(z_in)
 
+    for h in (0, first):
+        @pl.when(jnp.logical_not(y_recv[h]))
+        def _():
+            size = first if h == 0 else heads - first
+            y_in[pl.ds(h, size)] = jnp.zeros((size, DH, DH), F32)
+
     def remote(src, dst, send, recv, device):
         return pltpu.make_async_remote_copy(
             src_ref=src,
@@ -129,6 +143,37 @@
 
     position = (me * tokens + lax.broadcasted_iota(jnp.int32, (tokens, DH), 0)).astype(F32)
     scale = 1.0 / jnp.sqrt(DH * (position + 1.0))
+
+    def wait_plane(h):
+        @pl.when(has_prev)
+        def _():
+            z_copy(h).wait_recv()
+
+    def send_plane(h):
+        @pl.when(has_next)
+        def _():
+            z_copy(h).start()
+
+    def cross(h):
+        @pl.when(y_send[h])
+        def _():
+            y_copy(h).start()
+
+    def pass_on(h):
+        wait_plane(h)
+        here = state[core, h] + sib_in[h]
+        z_out[h] = z_in[h] + here
+        send_plane(h)
+        y_out[h] = z_in[h] + low * here
+        cross(h)
+
+    def chip_sum(h):
+        sib_copy(h).wait_recv()
+        if h < first:
+            y_out[h] = state[core, h] + sib_in[h]
+            cross(h)
+        else:
+            pl.when(jnp.logical_not(has_prev))(functools.partial(pass_on, h))
 
     for n, h in enumerate(order):
         for i in range(4):
@@ -142,6 +187,10 @@
                 barrier, 2 + has_prev.astype(jnp.int32) + has_next.astype(jnp.int32)
             )
         sib_copy(h).start()
+        if n >= 4:
+            chip_sum(order[n - 4])
+    for h in order[max(heads - 4, 0) :]:
+        chip_sum(h)
 
     def local(h):
         c = cols(h)
@@ -155,43 +204,30 @@
         acc_k[:, c] = dot(dscores, q, 0, 0)
         acc_v[:, c] = dot(scores, g, 0, 0)
 
-    for h in order:
-        sib_copy(h).wait_recv()
-        if h < first:
-            y_out[h] = state[core, h] + sib_in[h]
-            y_copy(h).start()
-
     def give(h, base):
         total[core, h] = base
         ret_out[h] = base + state[core, h]
         ret_copy(h).start()
 
-    def wait_plane(h):
-        @pl.when(has_prev)
-        def _():
-            z_copy(h).wait_recv()
-
-    def send_plane(h):
-        @pl.when(has_next)
-        def _():
-            z_copy(h).start()
-
     for h in range(first, heads):
-        wait_plane(h)
-        here = state[core, h] + sib_in[h]
-        z_out[h] = z_in[h] + here
-        send_plane(h)
-        y_out[h] = z_in[h] + low * here
-        y_copy(h).start()
+        pl.when(has_prev)(functools.partial(pass_on, h))
         local(h)
 
     for h in range(first):
-        y_copy(h).wait_recv()
+        @pl.when(y_recv[h])
+        def _():
+            y_copy(h).wait_recv()
+
         wait_plane(h)
         before = z_in[h]
-        z_out[h] = before + (y_out[h] + y_in[h])
-        send_plane(h)
-        give(h, before + high * y_in[h])
+        crossed = y_in[h]
+
+        @pl.when(has_next)
+        def _():
+            z_out[h] = before + (state[core, h] + sib_in[h] + crossed)
+            z_copy(h).start()
+
+        give(h, before + high * crossed)
         local(h)
 
     def finish(h):
@@ -205,19 +241,25 @@
         kg_ref[:, c] = (acc_k[:, c] + dot(v, suffix, 1, 1)).astype(BF16)
         vg_ref[:, c] = (acc_v[:, c] + dot(k, suffix, 1, 0)).astype(BF16)
 
-    for h in range(first, heads):
-        y_copy(h).wait_recv()
+    for n, h in enumerate(range(first, heads)):
+        @pl.when(y_recv[h])
+        def _():
+            y_copy(h).wait_recv()
+
         give(h, z_in[h] + y_in[h])
-        if h - first < first:
-            finish(h - first)
-
-    for h in range(first, heads):
+        for done in early[n]:
+            finish(done)
+
+    for h in rest:
         finish(h)
 
     for h in range(heads):
         sib_copy(h).wait_send()
-        y_copy(h).wait_send()
         ret_copy(h).wait_send()
+
+        @pl.when(y_send[h])
+        def _():
+            y_copy(h).wait_send()
 
         @pl.when(has_next)
         def _():

time: 26.3 us -> 25.6 us (0.973)
  Pallas kernels: 25.5 us -> 24.8 us
    pallas_call x1, Pallas kernels: 24.1 us -> 23.5 us  [body(): pl.pallas_call(functools.partial(kernel, planes, heads), out_shape=[out]...]
where the time goes in v3:
time: 25.6 us; the launch traced here: 25.5 us
  Pallas kernels  24.8 us (97%)
  between operations  0.64 us (2%)
    pallas_call x1, Pallas kernels, body(): pl.pallas_call(functools.partial(kernel, planes, heads), out_shape=[out]...  23.5 us
    pallas_call x1, Pallas kernels, body(): pl.pallas_call(store_kernel, out_shape=[out] * 4, in_specs=[pl.BlockSpec(...  1.35 us

profile of v3, /device:TPU:0, one launch (start us, length us, event | category | flops | bytes accessed | tf_op | source)
XLA Modules:
  0.0 25.5 jit_solution(4416346935406409306)
XLA Ops:
  0.6 23.5 %shard_map.75 = (bf16[256,1024]{1,0:T(8,128)(2,1)S(1)}, bf16[256,1024]{1,0:T(8,128)(2,1)S(1)}, bf16[256,1024]{1,0:T(8,128)(2,1)S(1)}, bf16[256,1024]{1,0:T(8,128)(2,1)S(1)}) custom-call(bf16[256,1024]{1,0:T(8,128)(2,1)} %q_hbm.1, bf16[256,1024]{1,0:T(8,128)(2,1)} %k_hbm.1, bf16[256,1024]{1,0:T(8,128)(2,1)} %v_hbm.1, bf16[256,1024]{1,0:T(8,128)(2,1)} %do_hbm.1), custom_call_target="tpu_custom_call" | custom-call | flops 1207959552 | bytes 4194304 | tf_op jit(solution)/shard_map/pallas_call | solution.py:289
  24.1 1.3 %shard_map.76 = (bf16[256,1024]{1,0:T(8,128)(2,1)}, bf16[256,1024]{1,0:T(8,128)(2,1)}, bf16[256,1024]{1,0:T(8,128)(2,1)}, bf16[256,1024]{1,0:T(8,128)(2,1)}) custom-call(bf16[256,1024]{1,0:T(8,128)(2,1)S(1)} %get-tuple-element.8.a_in, bf16[256,1024]{1,0:T(8,128)(2,1)S(1)} %get-tuple-element.9.q_in, bf16[256,1024]{1,0:T(8,128)(2,1)S(1)} %get-tuple-element.10.k_in, ...), custom_call_target="tpu_custom_call" | custom-call | tf_op jit(solution)/shard_map/pallas_call | solution.py:306

commit v4 on v3

--- a/solution.py
+++ b/solution.py
@@ -86,7 +86,7 @@
     def _():
         pl.semaphore_signal(barrier, inc=1, device_id=(group, me + step), device_id_type=MESH)
 
-    first = 3 * heads // 8
+    first = heads // 4
     order = [h for i in range(heads) for h in (i, first + i) if i < first or h >= first]
     order = [h for n, h in enumerate(order) if h < heads and h not in order[:n]]
 

time: 25.6 us -> 25.4 us (level)
  no operation moved by 1% of the time
where the time goes in v4:
time: 25.4 us; the launch traced here: 25.3 us
  Pallas kernels  24.6 us (97%)
  between operations  0.64 us (3%)
    pallas_call x1, Pallas kernels, body(): pl.pallas_call(functools.partial(kernel, planes, heads), out_shape=[out]...  23.3 us
    pallas_call x1, Pallas kernels, body(): pl.pallas_call(store_kernel, out_shape=[out] * 4, in_specs=[pl.BlockSpec(...  1.35 us

profile of v4, /device:TPU:0, one launch (start us, length us, event | category | flops | bytes accessed | tf_op | source)
XLA Modules:
  0.0 25.3 jit_solution(12927796593242765551)
XLA Ops:
  0.6 23.3 %shard_map.75 = (bf16[256,1024]{1,0:T(8,128)(2,1)S(1)}, bf16[256,1024]{1,0:T(8,128)(2,1)S(1)}, bf16[256,1024]{1,0:T(8,128)(2,1)S(1)}, bf16[256,1024]{1,0:T(8,128)(2,1)S(1)}) custom-call(bf16[256,1024]{1,0:T(8,128)(2,1)} %q_hbm.1, bf16[256,1024]{1,0:T(8,128)(2,1)} %k_hbm.1, bf16[256,1024]{1,0:T(8,128)(2,1)} %v_hbm.1, bf16[256,1024]{1,0:T(8,128)(2,1)} %do_hbm.1), custom_call_target="tpu_custom_call" | custom-call | flops 1207959552 | bytes 4194304 | tf_op jit(solution)/shard_map/pallas_call | solution.py:289
  23.9 1.3 %shard_map.76 = (bf16[256,1024]{1,0:T(8,128)(2,1)}, bf16[256,1024]{1,0:T(8,128)(2,1)}, bf16[256,1024]{1,0:T(8,128)(2,1)}, bf16[256,1024]{1,0:T(8,128)(2,1)}) custom-call(bf16[256,1024]{1,0:T(8,128)(2,1)S(1)} %get-tuple-element.8.a_in, bf16[256,1024]{1,0:T(8,128)(2,1)S(1)} %get-tuple-element.9.q_in, bf16[256,1024]{1,0:T(8,128)(2,1)S(1)} %get-tuple-element.10.k_in, ...), custom_call_target="tpu_custom_call" | custom-call | tf_op jit(solution)/shard_map/pallas_call | solution.py:306
